TPU v7x, 128 devices: a whole 4x4x4 slice. The times are simulated.
128 devices in a mesh: tile: 16 (over y_lo, x, core), mp: 8 (over y_hi, z).
Axes of the slice: x: 4, y: 4 (y_hi: 2, y_lo: 2; y = y_hi * 2 + y_lo), z: 4, core: 2. Of those that a mesh axis runs over, the one named last changes fastest.
Arguments:
- tokens: bfloat16 [128, 256, 1024], P('tile', 'mp'), may hold values from -6 to 6
- ln_gain_one: float32 [1024], replicated, may hold values from 0.5 to 1.5
- ln_gain_two: float32 [1024], replicated, may hold values from 0.5 to 1.5
- qkv_weight: bfloat16 [3, 1024, 1024], P(None, None, 'mp'), may hold values from -2 to 2
- out_weight: bfloat16 [1024, 1024], P('mp'), may hold values from -0.1875 to 0.1875
- in_weight: bfloat16 [4096, 1024], P('mp'), may hold values from -0.1875 to 0.1875
- mlp_out_weight: bfloat16 [4096, 1024], P('mp'), may hold values from -0.09375 to 0.09375
- proj_weight: bfloat16 [1024, 256], replicated, may hold values from -0.1875 to 0.1875
- land_mask: int32 [128], P('tile'), may hold values 0 or 1
- placement: int32 [128], replicated, may hold values from 0 to 127, as said below
- guide: bfloat16 [512, 256, 256], P(('tile', 'mp')), may hold values from -6 to 6
- conv_weights: bfloat16 [3, 3, 3, 256, 256], replicated, may hold values from -0.125 to 0.125
- conv_bias: float32 [3, 256], replicated, may hold values from -3 to 3
Outputs:
- dense_map: bfloat16 [512, 256, 256], P(('tile', 'mp'))
Inputs may be any that keep to these rules, and one draw needn't show every extreme that they name: placement is a permutation of the scene positions; the tiles of one group land in different slabs (entry // 8), so each slab receives at most one tile of each group.
All inputs are finite; a program needn't handle non-finite values. No bound on the sum of `land_mask` on one device may be relied on, other than what follows from the above.
Results may differ from a plain program's by a relative error of at most 0.018.
The roundings to bfloat16 on the way count: a program that leaves them out, or rounds other values in their place, can miss the bound.
Values may be sent and summed in bfloat16 or wider, within the bound.
No kernel may reach another device: no remote copies, remote signals or barrier semaphores. Data moves between devices by JAX's collectives and lax.ppermute only.
A program may use at most 128 MiB of HBM per device.

v0:
```python
import jax
import jax.numpy as jnp
from jax import lax
from jax.sharding import PartitionSpec as P

HEAD = 64
SIDE = 16
UP = 2
PATCHES = 256


def extended_2(block, sides, width):
    for axis, dim in sides:
        count = lax.axis_size(axis)
        forward = [(i, i + 1) for i in range(count - 1)]
        backward = [(target, source) for source, target in forward]
        low = lax.ppermute(
            lax.slice_in_dim(block, block.shape[dim] - width, None, axis=dim), axis, forward
        )
        high = lax.ppermute(lax.slice_in_dim(block, 0, width, axis=dim), axis, backward)
        block = jnp.concatenate([low, block, high], axis=dim)
    return block


def layer_norm(values, gain):
    widened = values.astype(jnp.float32)
    centre = jnp.mean(widened, axis=-1, keepdims=True)
    spread = jnp.mean((widened - centre) ** 2, axis=-1, keepdims=True)
    return ((widened - centre) * lax.rsqrt(spread + 1e-06) * gain).astype(jnp.bfloat16)


def conv_layer(extended, kernel, shift, out_count):
    width_px = extended.shape[1]
    padded = jnp.pad(extended, ((0, 0), (1, 1), (0, 0)))
    running = jnp.zeros((out_count, width_px, kernel.shape[-1]), jnp.float32) + shift
    for row_shift in range(3):
        for col_shift in range(3):
            window = padded[row_shift : row_shift + out_count, col_shift : col_shift + width_px]
            running = running + jnp.einsum(
                "rwc,cd->rwd",
                window,
                kernel[row_shift, col_shift],
                preferred_element_type=jnp.float32,
            )
    return running


def per_device(
    tokens,
    ln_gain_one,
    ln_gain_two,
    qkv_weight,
    out_weight,
    in_weight,
    mlp_out_weight,
    proj_weight,
    land_mask,
    placement,
    guide,
    conv_weights,
    conv_bias,
):
    tiles_here = tokens.shape[0]
    seg_rows = tokens.shape[1]
    groups = lax.axis_size("tile")
    normed = layer_norm(tokens, ln_gain_one)
    gathered = lax.all_gather(normed, "mp", axis=1, tiled=True)
    projected = jnp.einsum(
        "tpd,kde->ktpe", gathered, qkv_weight, preferred_element_type=jnp.float32
    ).astype(jnp.bfloat16)
    heads_local = projected.shape[-1] // HEAD
    shaped = projected.reshape(3, tiles_here, PATCHES, heads_local, HEAD)
    scores = jnp.einsum(
        "tphe,tqhe->thpq", shaped[0], shaped[1], preferred_element_type=jnp.float32
    ) * HEAD ** (-0.5)
    soft_weights = jax.nn.softmax(scores, axis=-1).astype(jnp.bfloat16)
    context = jnp.einsum(
        "thpq,tqhe->tphe", soft_weights, shaped[2], preferred_element_type=jnp.float32
    )
    context = context.astype(jnp.bfloat16).reshape(tiles_here, PATCHES, heads_local * HEAD)
    partial_value = jnp.einsum(
        "tpe,ed->tpd", context, out_weight, preferred_element_type=jnp.float32
    )
    attention = lax.psum_scatter(
        partial_value.astype(jnp.bfloat16), "mp", scatter_dimension=1, tiled=True
    ).astype(jnp.float32)
    middle = (tokens.astype(jnp.float32) + attention).astype(jnp.bfloat16)
    normed_mid = layer_norm(middle, ln_gain_two)
    gathered_mid = lax.all_gather(normed_mid, "mp", axis=1, tiled=True)
    hidden = jnp.einsum("tpd,fd->tpf", gathered_mid, in_weight, preferred_element_type=jnp.float32)
    hidden = jax.nn.gelu(hidden).astype(jnp.bfloat16)
    mlp_terms = jnp.einsum(
        "tpf,fd->tpd", hidden, mlp_out_weight, preferred_element_type=jnp.float32
    )
    mlp_part = lax.psum_scatter(
        mlp_terms.astype(jnp.bfloat16), "mp", scatter_dimension=1, tiled=True
    ).astype(jnp.float32)
    features = (middle.astype(jnp.float32) + mlp_part).astype(jnp.bfloat16)
    mask_here = land_mask.astype(jnp.bfloat16)[:, None, None]
    group_here = lax.axis_index("tile")
    slab_all = placement // tiles_here
    column_all = placement % tiles_here
    group_all = jnp.arange(placement.shape[0], dtype=jnp.int32) // tiles_here
    slab_local = lax.dynamic_slice_in_dim(slab_all, group_here * tiles_here, tiles_here, 0)
    selector = (slab_local[None, :] == jnp.arange(groups, dtype=jnp.int32)[:, None]).astype(
        jnp.bfloat16
    )
    in_slab = slab_all == group_here
    column_hot = (
        column_all[:, None] == jnp.arange(tiles_here, dtype=jnp.int32)[None, :]
    ) & in_slab[:, None]
    group_hot = group_all[:, None] == jnp.arange(groups, dtype=jnp.int32)[None, :]
    arrange = jnp.einsum(
        "tk,tg->kg", column_hot.astype(jnp.float32), group_hot.astype(jnp.float32)
    ).astype(jnp.bfloat16)
    masked = features * mask_here
    outgoing = jnp.einsum(
        "sj,jpd->spd", selector, masked, preferred_element_type=jnp.float32
    ).astype(jnp.bfloat16)
    incoming = lax.all_to_all(outgoing, "tile", split_axis=0, concat_axis=0, tiled=True)
    slab_feats = jnp.einsum(
        "kg,gpd->kpd", arrange, incoming, preferred_element_type=jnp.float32
    ).astype(jnp.bfloat16)
    slab_embed = jnp.einsum(
        "kpd,dc->kpc", slab_feats, proj_weight, preferred_element_type=jnp.float32
    )
    slab_embed = slab_embed.astype(jnp.bfloat16)
    token_rows = seg_rows // SIDE
    channels = proj_weight.shape[1]
    image = slab_embed.reshape(tiles_here, token_rows, SIDE, channels)
    image = jnp.transpose(image, (1, 0, 2, 3)).reshape(token_rows, tiles_here * SIDE, channels)
    upsampled = jnp.repeat(jnp.repeat(image, UP, axis=0), UP, axis=1)
    guided = (upsampled.astype(jnp.float32) + guide.astype(jnp.float32)).astype(jnp.bfloat16)
    row_count = guided.shape[0]

    def section(values, layer):
        widened = extended_2(values, ((("tile", "mp"), 0),), 1)
        return conv_layer(widened, conv_weights[layer], conv_bias[layer], row_count)

    first = jax.nn.gelu(section(guided, 0)).astype(jnp.bfloat16)
    second = jax.nn.gelu(section(first, 1)).astype(jnp.bfloat16)
    last_term = section(second, 2)
    return (guided.astype(jnp.float32) + last_term).astype(jnp.bfloat16)


def solution(mesh):
    in_specs = (
        P("tile", "mp", None),
        P(),
        P(),
        P(None, None, "mp"),
        P("mp", None),
        P("mp", None),
        P("mp", None),
        P(),
        P("tile"),
        P(),
        P(("tile", "mp"), None, None),
        P(),
        P(),
    )
    out_specs = P(("tile", "mp"), None, None)
    return jax.shard_map(
        per_device, mesh=mesh, in_specs=in_specs, out_specs=out_specs, check_vma=False
    )
```

profile of v0, /device:TPU:1, one launch (start us, length us, event | category | flops | bytes accessed | tf_op | source)
XLA Modules:
  0.0 432.7 jit_solution(2327485380840038039)
XLA Ops:
  6.5 1.3 convert_reduce_fusion.1
  7.9 1.3 fusion.59
  9.2 2.1 fusion.61
  11.4 74.5 %all-gather.3.cloned.1.call-done = bf16[8,256,1024]{2,1,0:T(8,128)(2,1)} async-done(((bf16[8,32,1024]{2,1,0:T(8,128)(2,1)}), bf16[8,256,1024]{2,1,0:T(8,128)(2,1)}) %all-gather.3.cloned.1.call-update) | async-done | bytes 4194320 | tf_op jit(solution)/shard_map/all_gather | solution.py:67
  85.9 4.0 fusion.25
  90.1 3.5 fusion.186
  93.6 2.7 fusion.48
  96.3 3.2 convolution_convert_fusion.1
  99.7 81.9 %reduce-scatter.3.cloned.1.call-done = bf16[8,32,1024]{2,1,0:T(8,128)(2,1)} async-done(((bf16[8,256,1024]{2,1,0:T(8,128)(2,1)}), bf16[8,32,1024]{2,1,0:T(8,128)(2,1)}) %reduce-scatter.3.cloned.1.call-update) | async-done | bytes 524304 | tf_op jit(solution)/shard_map/reduce_scatter | solution.py:84
  181.6 1.3 convert_reduce_fusion
  183.1 1.1 fusion.58
  184.3 71.1 %all-gather.5.cloned.1.call-done = bf16[8,256,1024]{2,1,0:T(8,128)(2,1)} async-done(((bf16[8,32,1024]{2,1,0:T(8,128)(2,1)}), bf16[8,256,1024]{2,1,0:T(8,128)(2,1)}) %all-gather.5.cloned.1.call-update) | async-done | bytes 4194320 | tf_op jit(solution)/shard_map/all_gather | solution.py:89
  255.4 8.2 %convolution_convert_fusion = bf16[8,256,1024]{2,1,0:T(8,128)(2,1)} fusion(bf16[8,256,1024]{2,1,0:T(8,128)(2,1)} %all-gather.5.cloned.1.call-done, bf16[512,1024]{1,0:T(8,128)(2,1)S(1)} %copy-done, bf16[512,1024]{1,0:T(8,128)(2,1)S(1)} %copy-done.8), kind=kOutput, calls=%fused_computation.16 | convolution fusion | flops 4306501632 | bytes 10485760 | tf_op jit(solution)/shard_map/tpf,fd->tpd/dot_general | solution.py:92
  263.6 0.6 copy-done.10
  264.4 81.3 %reduce-scatter.5.cloned.1.call-done = bf16[8,32,1024]{2,1,0:T(8,128)(2,1)} async-done(((bf16[8,256,1024]{2,1,0:T(8,128)(2,1)}), bf16[8,32,1024]{2,1,0:T(8,128)(2,1)}) %reduce-scatter.5.cloned.1.call-update) | async-done | bytes 524304 | tf_op jit(solution)/shard_map/reduce_scatter | solution.py:95
  345.7 1.3 fusion.114
  346.9 0.5 fusion.149
  347.4 1.5 copy.37
  349.0 6.1 %all-to-all-start = ((bf16[16,32,1024]{2,1,0:T(8,128)(2,1)}), bf16[16,32,1024]{2,1,0:T(8,128)(2,1)S(1)}, u32[]{:S(2)}, u32[]{:S(2)}) async-start(bf16[16,32,1024]{2,1,0:T(8,128)(2,1)} %copy.37), calls=%async_computation.2 | async-start | bytes 2097152 | tf_op jit(solution)/shard_map/all_to_all | solution.py:120
  355.1 3.3 slice_bitcast_fusion
  358.4 12.5 %all-to-all-done = bf16[16,32,1024]{2,1,0:T(8,128)(2,1)S(1)} async-done(((bf16[16,32,1024]{2,1,0:T(8,128)(2,1)}), bf16[16,32,1024]{2,1,0:T(8,128)(2,1)S(1)}, u32[]{:S(2)}, u32[]{:S(2)}) %all-to-all-start) | async-done | bytes 1048608 | tf_op jit(solution)/shard_map/all_to_all | solution.py:120
  370.9 1.7 fusion.83
  372.6 1.7 convolution_convert_fusion.2
  374.3 0.4 broadcast_in_dim.5
  374.7 1.7 convert_element_type.132
  376.4 1.6 add_convert_fusion
  378.0 2.9 collective-permute-start
  380.8 6.3 %collective-permute-start.1 = (bf16[1,256,256]{2,1,0:T(8,128)(2,1)S(1)}, bf16[1,256,256]{2,1,0:T(8,128)(2,1)S(1)}, u32[]{:S(2)}, u32[]{:S(2)}) collective-permute-start(bf16[1,256,256]{2,1,0:T(8,128)(2,1)S(1)} %get-tuple-element.20), channel_id=1, source_target_pairs={{1,0},{2,1},{3,2},{4,3},{5,4},{6,5},{7,6},{8,7},{9,8},{10,9},{11,1... | collective-permute-start | bytes 393224 | tf_op jit(solution)/shard_map/ppermute | solution.py:20
  387.5 0.4 collective-permute-done
  387.9 2.6 collective-permute-done.1
  391.0 0.3 fusion.141
  391.6 0.3 fusion.145
  391.9 0.3 fusion.137
  392.5 0.5 fusion.46
  393.0 0.6 fusion.71
  393.6 1.9 collective-permute-start.2
  395.6 8.0 %collective-permute-start.3 = (bf16[1,256,256]{2,1,0:T(8,128)(2,1)S(1)}, bf16[1,256,256]{2,1,0:T(8,128)(2,1)S(1)}, u32[]{:S(2)}, u32[]{:S(2)}) collective-permute-start(bf16[1,256,256]{2,1,0:T(8,128)(2,1)S(1)} %get-tuple-element.18), channel_id=1, source_target_pairs={{1,0},{2,1},{3,2},{4,3},{5,4},{6,5},{7,6},{8,7},{9,8},{10,9},{11,1... | collective-permute-start | bytes 393224 | tf_op jit(solution)/shard_map/ppermute | solution.py:20
  403.9 0.4 collective-permute-done.2
  404.3 2.3 collective-permute-done.3
  408.6 0.5 fusion.40
  409.1 0.6 fusion.79
  409.7 1.9 collective-permute-start.4
  411.6 8.0 %collective-permute-start.5 = (bf16[1,256,256]{2,1,0:T(8,128)(2,1)S(1)}, bf16[1,256,256]{2,1,0:T(8,128)(2,1)S(1)}, u32[]{:S(2)}, u32[]{:S(2)}) collective-permute-start(bf16[1,256,256]{2,1,0:T(8,128)(2,1)S(1)} %get-tuple-element.16), channel_id=1, source_target_pairs={{1,0},{2,1},{3,2},{4,3},{5,4},{6,5},{7,6},{8,7},{9,8},{10,9},{11,1... | collective-permute-start | bytes 393224 | tf_op jit(solution)/shard_map/ppermute | solution.py:20
  419.9 0.4 collective-permute-done.4
  420.3 2.2 collective-permute-done.5
  423.0 0.3 fusion.123
  424.6 0.5 fusion.34
  425.1 1.1 fusion.47
  (65 shorter events, 6.6 us)
Async XLA Ops:
  6.5 248.8 %copy-start = (bf16[512,1024]{1,0:T(8,128)(2,1)S(1)}, bf16[512,1024]{1,0:T(8,128)(2,1)}, u32[]{:S(2)}) copy-start(bf16[512,1024]{1,0:T(8,128)(2,1)} %param.19) | copy-start | bytes 3145732
  6.5 79.4 %copy-start.9 = (bf16[3,1024,128]{2,1,0:T(8,128)(2,1)S(1)}, bf16[3,1024,128]{2,1,0:T(8,128)(2,1)}, u32[]{:S(2)}) copy-start(bf16[3,1024,128]{2,1,0:T(8,128)(2,1)} %param.16) | copy-start | bytes 2359300
  6.5 79.4 %all-gather.3.cloned.1.call-start = ((), (), s32[]{:S(2)}) async-start(), calls=%async_computation.3 | async-start | bytes 4718592 | tf_op jit(solution)/shard_map/all_gather | solution.py:67
  11.4 170.2 %reduce-scatter.3.cloned.1.call-start = ((), (), s32[]{:S(2)}) async-start(), calls=%async_computation.4 | async-start | bytes 4718592 | tf_op jit(solution)/shard_map/reduce_scatter | solution.py:84
  93.6 2.7 copy-start.4
  99.6 82.0 %copy-start.2 = (bf16[8,32,1024]{2,1,0:T(8,128)(2,1)S(1)}, bf16[8,32,1024]{2,1,0:T(8,128)(2,1)}, u32[]{:S(2)}) copy-start(bf16[8,32,1024]{2,1,0:T(8,128)(2,1)} %param.13) | copy-start | bytes 1572868
  99.6 83.5 %copy-start.5 = (f32[1024]{0:T(1024)S(1)}, f32[1024]{0:T(1024)}, u32[]{:S(2)}) copy-start(f32[1024]{0:T(1024)} %param.15) | copy-start | bytes 12292
  99.6 155.8 %copy-start.8 = (bf16[512,1024]{1,0:T(8,128)(2,1)S(1)}, bf16[512,1024]{1,0:T(8,128)(2,1)}, u32[]{:S(2)}) copy-start(bf16[512,1024]{1,0:T(8,128)(2,1)} %param.18) | copy-start | bytes 3145732
  99.6 155.8 %all-gather.5.cloned.1.call-start = ((), (), s32[]{:S(2)}) async-start(), calls=%async_computation.5 | async-start | bytes 4718592 | tf_op jit(solution)/shard_map/all_gather | solution.py:89
  184.3 161.4 %reduce-scatter.5.cloned.1.call-start = ((), (), s32[]{:S(2)}) async-start(), calls=%async_computation.6 | async-start | bytes 4718592 | tf_op jit(solution)/shard_map/reduce_scatter | solution.py:95
  263.6 0.7 copy-start.10
  263.6 0.7 copy-start.7
  349.0 6.1 %copy-start.6 = (f32[3,256]{1,0:T(4,128)S(1)}, f32[3,256]{1,0:T(4,128)}, u32[]{:S(2)}) copy-start(f32[3,256]{1,0:T(4,128)} %param.25) | copy-start | bytes 9220
  349.0 21.9 %all-to-all-start = ((bf16[16,32,1024]{2,1,0:T(8,128)(2,1)}), bf16[16,32,1024]{2,1,0:T(8,128)(2,1)S(1)}, u32[]{:S(2)}, u32[]{:S(2)}) async-start(bf16[16,32,1024]{2,1,0:T(8,128)(2,1)} %copy.37), calls=%async_computation.2 | async-start | bytes 2097152 | tf_op jit(solution)/shard_map/all_to_all | solution.py:120
  376.4 10.8 %copy-start.3 = (bf16[3,3,256,256]{3,2,1,0:T(8,128)(2,1)S(1)}, bf16[3,3,256,256]{3,2,1,0:T(8,128)(2,1)}, u32[]{:S(2)}) copy-start(bf16[3,3,256,256]{3,2,1,0:T(8,128)(2,1)} %get-tuple-element.10) | copy-start | bytes 3538948
  378.0 9.9 %collective-permute-start = (bf16[1,256,256]{2,1,0:T(8,128)(2,1)S(1)}, bf16[1,256,256]{2,1,0:T(8,128)(2,1)S(1)}, u32[]{:S(2)}, u32[]{:S(2)}) collective-permute-start(bf16[1,256,256]{2,1,0:T(8,128)(2,1)S(1)} %get-tuple-element.19), channel_id=1, source_target_pairs={{0,1},{1,2},{2,3},{3,4},{4,5},{5,6},{6,7},{7,8},{8,9},{9,10},{10,1... | collective-permute-start | bytes 393224 | tf_op jit(solution)/shard_map/ppermute | solution.py:17
  380.8 9.6 %collective-permute-start.1 = (bf16[1,256,256]{2,1,0:T(8,128)(2,1)S(1)}, bf16[1,256,256]{2,1,0:T(8,128)(2,1)S(1)}, u32[]{:S(2)}, u32[]{:S(2)}) collective-permute-start(bf16[1,256,256]{2,1,0:T(8,128)(2,1)S(1)} %get-tuple-element.20), channel_id=1, source_target_pairs={{1,0},{2,1},{3,2},{4,3},{5,4},{6,5},{7,6},{8,7},{9,8},{10,9},{11,1... | collective-permute-start | bytes 393224 | tf_op jit(solution)/shard_map/ppermute | solution.py:20
  393.6 10.6 %collective-permute-start.2 = (bf16[1,256,256]{2,1,0:T(8,128)(2,1)S(1)}, bf16[1,256,256]{2,1,0:T(8,128)(2,1)S(1)}, u32[]{:S(2)}, u32[]{:S(2)}) collective-permute-start(bf16[1,256,256]{2,1,0:T(8,128)(2,1)S(1)} %get-tuple-element.17), channel_id=1, source_target_pairs={{0,1},{1,2},{2,3},{3,4},{4,5},{5,6},{6,7},{7,8},{8,9},{9,10},{10,1... | collective-permute-start | bytes 393224 | tf_op jit(solution)/shard_map/ppermute | solution.py:17
  395.6 11.0 %collective-permute-start.3 = (bf16[1,256,256]{2,1,0:T(8,128)(2,1)S(1)}, bf16[1,256,256]{2,1,0:T(8,128)(2,1)S(1)}, u32[]{:S(2)}, u32[]{:S(2)}) collective-permute-start(bf16[1,256,256]{2,1,0:T(8,128)(2,1)S(1)} %get-tuple-element.18), channel_id=1, source_target_pairs={{1,0},{2,1},{3,2},{4,3},{5,4},{6,5},{7,6},{8,7},{9,8},{10,9},{11,1... | collective-permute-start | bytes 393224 | tf_op jit(solution)/shard_map/ppermute | solution.py:20
  409.7 10.6 %collective-permute-start.4 = (bf16[1,256,256]{2,1,0:T(8,128)(2,1)S(1)}, bf16[1,256,256]{2,1,0:T(8,128)(2,1)S(1)}, u32[]{:S(2)}, u32[]{:S(2)}) collective-permute-start(bf16[1,256,256]{2,1,0:T(8,128)(2,1)S(1)} %get-tuple-element.15), channel_id=1, source_target_pairs={{0,1},{1,2},{2,3},{3,4},{4,5},{5,6},{6,7},{7,8},{8,9},{9,10},{10,1... | collective-permute-start | bytes 393224 | tf_op jit(solution)/shard_map/ppermute | solution.py:17
  411.6 10.9 %collective-permute-start.5 = (bf16[1,256,256]{2,1,0:T(8,128)(2,1)S(1)}, bf16[1,256,256]{2,1,0:T(8,128)(2,1)S(1)}, u32[]{:S(2)}, u32[]{:S(2)}) collective-permute-start(bf16[1,256,256]{2,1,0:T(8,128)(2,1)S(1)} %get-tuple-element.16), channel_id=1, source_target_pairs={{1,0},{2,1},{3,2},{4,3},{5,4},{6,5},{7,6},{8,7},{9,8},{10,9},{11,1... | collective-permute-start | bytes 393224 | tf_op jit(solution)/shard_map/ppermute | solution.py:20
  424.6 1.6 copy-start.1
Sparse Core Ops, SparseCore 0:
  11.5 74.3 all-gather.2
  99.7 81.7 reduce-scatter.2
  184.4 70.9 all-gather.4
  263.7 81.8 reduce-scatter.4
where the time goes:
time: 433 us
  waiting for transfers between devices  330 us (76%)
  matrix products  35.6 us (8%)
  starting transfers between devices  35.2 us (8%)
  between operations  13.5 us (3%)
  other arithmetic  10.9 us (3%)
  local copies, waits for them, and re-layouts  7.92 us (2%)
    reduce_scatter x1, waiting for transfers between devices, per_device(): lax.psum_scatter(partial_value.astype(jnp.bfloat16), 'mp', scatter_dimens...  81.9 us
    reduce_scatter x1, waiting for transfers between devices, per_device(): lax.psum_scatter(mlp_terms.astype(jnp.bfloat16), 'mp', scatter_dimension=...  81.3 us
    all_gather x1, waiting for transfers between devices, per_device(): gathered = lax.all_gather(normed, 'mp', axis=1, tiled=True)  74.5 us
    all_gather x1, waiting for transfers between devices, per_device(): gathered_mid = lax.all_gather(normed_mid, 'mp', axis=1, tiled=True)  71.1 us
    ppermute x3, starting transfers between devices, extended_2(): lax.ppermute(lax.slice_in_dim(block, 0, width, axis=dim), axis, backward)  22.3 us
    all_to_all x1, waiting for transfers between devices, per_device(): lax.all_to_all(outgoing, 'tile', split_axis=0, concat_axis=0, tiled=True)  12.5 us
    dot_general x27, matrix products, conv_layer(): jnp.einsum('rwc,cd->rwd', window, kernel[row_shift, col_shift], preferred...  10.1 us
  transfers between devices with their start and end apart: 11, of which 11 were waited for; matrix products, arithmetic and copies ran while one was open for 1% of the time, Pallas kernels for 0%

commit v1 on v0

--- a/solution.py
+++ b/solution.py
@@ -86,7 +86,8 @@
     ).astype(jnp.float32)
     middle = (tokens.astype(jnp.float32) + attention).astype(jnp.bfloat16)
     normed_mid = layer_norm(middle, ln_gain_two)
-    gathered_mid = lax.all_gather(normed_mid, "mp", axis=1, tiled=True)
+    repeated = jnp.stack([normed_mid] * lax.axis_size("mp"))
+    gathered_mid = jnp.concatenate(lax.all_to_all(repeated, "mp", 0, 0), axis=1)
     hidden = jnp.einsum("tpd,fd->tpf", gathered_mid, in_weight, preferred_element_type=jnp.float32)
     hidden = jax.nn.gelu(hidden).astype(jnp.bfloat16)
     mlp_terms = jnp.einsum(

time: 433 us -> 417 us (0.963)
  waiting for transfers between devices: 330 us -> 262 us
  blocking collectives: 0 us -> 49.9 us
    all_gather x1 -> x0, waiting for transfers between devices: 71.1 us -> none  [per_device(): gathered_mid = lax.all_gather(normed_mid, 'mp', axis=1, tiled=True)]
    all_to_all x0 -> x1, blocking collectives: none -> 49.9 us  [per_device(): gathered_mid = jnp.concatenate(lax.all_to_all(repeated, 'mp', 0, 0), axis=1)]
  transfers between devices with their start and end apart: 11 -> 10, of which waited for: 11 -> 10; matrix products, arithmetic and copies ran while one was open for 1% -> 1% of each run, Pallas kernels for 0% -> 0%
where the time goes in v1:
time: 417 us
  waiting for transfers between devices  262 us (63%)
  blocking collectives  49.9 us (12%)
  matrix products  35.7 us (9%)
  starting transfers between devices  35.1 us (8%)
  between operations  13.5 us (3%)
  local copies, waits for them, and re-layouts  10.9 us (3%)
  other arithmetic  10.1 us (2%)
    reduce_scatter x1, waiting for transfers between devices, per_device(): lax.psum_scatter(mlp_terms.astype(jnp.bfloat16), 'mp', scatter_dimension=...  84.5 us
    reduce_scatter x1, waiting for transfers between devices, per_device(): lax.psum_scatter(partial_value.astype(jnp.bfloat16), 'mp', scatter_dimens...  81.9 us
    all_gather x1, waiting for transfers between devices, per_device(): gathered = lax.all_gather(normed, 'mp', axis=1, tiled=True)  74.5 us
    all_to_all x1, blocking collectives, per_device(): gathered_mid = jnp.concatenate(lax.all_to_all(repeated, 'mp', 0, 0), axis=1)  49.9 us
    ppermute x3, starting transfers between devices, extended_2(): lax.ppermute(lax.slice_in_dim(block, 0, width, axis=dim), axis, backward)  22.3 us
    all_to_all x1, waiting for transfers between devices, per_device(): lax.all_to_all(outgoing, 'tile', split_axis=0, concat_axis=0, tiled=True)  12.5 us
    dot_general x27, matrix products, conv_layer(): jnp.einsum('rwc,cd->rwd', window, kernel[row_shift, col_shift], preferred...  10 us
  transfers between devices with their start and end apart: 10, of which 10 were waited for; matrix products, arithmetic and copies ran while one was open for 1% of the time, Pallas kernels for 0%

profile of v1, /device:TPU:1, one launch (start us, length us, event | category | flops | bytes accessed | tf_op | source)
XLA Modules:
  0.0 416.8 jit_solution(528101683971343547)
XLA Ops:
  6.5 1.3 convert_reduce_fusion.1
  7.9 1.3 fusion.59
  9.2 2.1 fusion.61
  11.4 74.5 %all-gather.2.cloned.1.call-done = bf16[8,256,1024]{2,1,0:T(8,128)(2,1)} async-done(((bf16[8,32,1024]{2,1,0:T(8,128)(2,1)}), bf16[8,256,1024]{2,1,0:T(8,128)(2,1)}) %all-gather.2.cloned.1.call-update) | async-done | bytes 4194320 | tf_op jit(solution)/shard_map/all_gather | solution.py:67
  85.9 4.0 fusion.25
  90.1 3.5 fusion.185
  93.6 2.7 fusion.48
  96.3 3.2 convolution_convert_fusion.1
  99.6 81.9 %reduce-scatter.3.cloned.1.call-done = bf16[8,32,1024]{2,1,0:T(8,128)(2,1)} async-done(((bf16[8,256,1024]{2,1,0:T(8,128)(2,1)}), bf16[8,32,1024]{2,1,0:T(8,128)(2,1)}) %reduce-scatter.3.cloned.1.call-update) | async-done | bytes 524304 | tf_op jit(solution)/shard_map/reduce_scatter | solution.py:84
  181.5 1.3 convert_reduce_fusion
  183.4 0.5 stack.2
  183.9 49.9 %all_to_all.10 = bf16[8,8,32,1024]{3,2,1,0:T(8,128)(2,1)S(1)} all-to-all(bf16[8,8,32,1024]{3,2,1,0:T(8,128)(2,1)S(1)} %stack.2), channel_id=1, replica_groups=mesh['tile'=16,'mp'=8] {'mp'}, dimensions={0} | all-to-all | bytes 8388608 | tf_op jit(solution)/shard_map/all_to_all | solution.py:90
  233.9 2.4 copy.31
  236.3 8.3 %convolution_convert_fusion = bf16[8,256,1024]{2,1,0:T(8,128)(2,1)} fusion(bf16[8,256,1024]{2,1,0:T(8,128)(2,1)} %bitcast.203, bf16[512,1024]{1,0:T(8,128)(2,1)S(1)} %copy-done, bf16[512,1024]{1,0:T(8,128)(2,1)S(1)} %copy-done.8), kind=kOutput, calls=%fused_computation.16 | convolution fusion | flops 4306501632 | bytes 10485760 | tf_op jit(solution)/shard_map/tpf,fd->tpd/dot_general | solution.py:93
  244.6 0.6 copy-done.10
  245.3 84.5 %reduce-scatter.5.cloned.1.call-done = bf16[8,32,1024]{2,1,0:T(8,128)(2,1)} async-done(((bf16[8,256,1024]{2,1,0:T(8,128)(2,1)}), bf16[8,32,1024]{2,1,0:T(8,128)(2,1)}) %reduce-scatter.5.cloned.1.call-update) | async-done | bytes 524304 | tf_op jit(solution)/shard_map/reduce_scatter | solution.py:96
  329.8 1.3 fusion.113
  331.0 0.6 convolution_convert_fusion.2
  331.6 1.5 copy.33
  333.2 6.0 %all-to-all-start.1 = ((bf16[16,32,1024]{2,1,0:T(8,128)(2,1)}), bf16[16,32,1024]{2,1,0:T(8,128)(2,1)S(1)}, u32[]{:S(2)}, u32[]{:S(2)}) async-start(bf16[16,32,1024]{2,1,0:T(8,128)(2,1)} %copy.33), calls=%async_computation.3 | async-start | bytes 2097152 | tf_op jit(solution)/shard_map/all_to_all | solution.py:121
  339.2 3.3 slice_bitcast_fusion
  342.5 12.5 %all-to-all-done.1 = bf16[16,32,1024]{2,1,0:T(8,128)(2,1)S(1)} async-done(((bf16[16,32,1024]{2,1,0:T(8,128)(2,1)}), bf16[16,32,1024]{2,1,0:T(8,128)(2,1)S(1)}, u32[]{:S(2)}, u32[]{:S(2)}) %all-to-all-start.1) | async-done | bytes 1048608 | tf_op jit(solution)/shard_map/all_to_all | solution.py:121
  355.0 1.7 convolution_convert_fusion.3
  356.7 1.7 convolution_convert_fusion.4
  358.4 0.4 broadcast_in_dim.5
  358.8 1.7 convert_element_type.132
  360.5 1.6 add_convert_fusion
  362.1 2.9 collective-permute-start
  365.0 6.2 %collective-permute-start.1 = (bf16[1,256,256]{2,1,0:T(8,128)(2,1)S(1)}, bf16[1,256,256]{2,1,0:T(8,128)(2,1)S(1)}, u32[]{:S(2)}, u32[]{:S(2)}) collective-permute-start(bf16[1,256,256]{2,1,0:T(8,128)(2,1)S(1)} %get-tuple-element.20), channel_id=1, source_target_pairs={{1,0},{2,1},{3,2},{4,3},{5,4},{6,5},{7,6},{8,7},{9,8},{10,9},{11,1... | collective-permute-start | bytes 393224 | tf_op jit(solution)/shard_map/ppermute | solution.py:20
  371.6 0.4 collective-permute-done
  372.0 2.6 collective-permute-done.1
  375.7 0.3 fusion.144
  376.0 0.3 fusion.136
  376.6 0.5 fusion.46
  377.1 0.6 fusion.71
  377.7 1.9 collective-permute-start.2
  379.7 8.0 %collective-permute-start.3 = (bf16[1,256,256]{2,1,0:T(8,128)(2,1)S(1)}, bf16[1,256,256]{2,1,0:T(8,128)(2,1)S(1)}, u32[]{:S(2)}, u32[]{:S(2)}) collective-permute-start(bf16[1,256,256]{2,1,0:T(8,128)(2,1)S(1)} %get-tuple-element.18), channel_id=1, source_target_pairs={{1,0},{2,1},{3,2},{4,3},{5,4},{6,5},{7,6},{8,7},{9,8},{10,9},{11,1... | collective-permute-start | bytes 393224 | tf_op jit(solution)/shard_map/ppermute | solution.py:20
  388.0 0.4 collective-permute-done.2
  388.4 2.3 collective-permute-done.3
  391.5 0.3 fusion.129
  392.7 0.5 fusion.40
  393.2 0.6 fusion.79
  393.8 1.9 collective-permute-start.4
  395.7 8.0 %collective-permute-start.5 = (bf16[1,256,256]{2,1,0:T(8,128)(2,1)S(1)}, bf16[1,256,256]{2,1,0:T(8,128)(2,1)S(1)}, u32[]{:S(2)}, u32[]{:S(2)}) collective-permute-start(bf16[1,256,256]{2,1,0:T(8,128)(2,1)S(1)} %get-tuple-element.16), channel_id=1, source_target_pairs={{1,0},{2,1},{3,2},{4,3},{5,4},{6,5},{7,6},{8,7},{9,8},{10,9},{11,1... | collective-permute-start | bytes 393224 | tf_op jit(solution)/shard_map/ppermute | solution.py:20
  404.0 0.4 collective-permute-done.4
  404.4 2.2 collective-permute-done.5
  408.7 0.5 fusion.34
  409.1 1.1 fusion.47
  (65 shorter events, 7.1 us)
Async XLA Ops:
  6.5 229.7 %copy-start = (bf16[512,1024]{1,0:T(8,128)(2,1)S(1)}, bf16[512,1024]{1,0:T(8,128)(2,1)}, u32[]{:S(2)}) copy-start(bf16[512,1024]{1,0:T(8,128)(2,1)} %param.19) | copy-start | bytes 3145732
  6.5 79.4 %copy-start.9 = (bf16[3,1024,128]{2,1,0:T(8,128)(2,1)S(1)}, bf16[3,1024,128]{2,1,0:T(8,128)(2,1)}, u32[]{:S(2)}) copy-start(bf16[3,1024,128]{2,1,0:T(8,128)(2,1)} %param.16) | copy-start | bytes 2359300
  6.5 79.4 %all-gather.2.cloned.1.call-start = ((), (), s32[]{:S(2)}) async-start(), calls=%async_computation.4 | async-start | bytes 4718592 | tf_op jit(solution)/shard_map/all_gather | solution.py:67
  11.4 170.2 %reduce-scatter.3.cloned.1.call-start = ((), (), s32[]{:S(2)}) async-start(), calls=%async_computation.5 | async-start | bytes 4718592 | tf_op jit(solution)/shard_map/reduce_scatter | solution.py:84
  93.6 2.7 copy-start.4
  99.5 82.0 %copy-start.2 = (bf16[8,32,1024]{2,1,0:T(8,128)(2,1)S(1)}, bf16[8,32,1024]{2,1,0:T(8,128)(2,1)}, u32[]{:S(2)}) copy-start(bf16[8,32,1024]{2,1,0:T(8,128)(2,1)} %param.13) | copy-start | bytes 1572868
  99.6 83.5 %copy-start.5 = (f32[1024]{0:T(1024)S(1)}, f32[1024]{0:T(1024)}, u32[]{:S(2)}) copy-start(f32[1024]{0:T(1024)} %param.15) | copy-start | bytes 12292
  99.6 230.2 %reduce-scatter.5.cloned.1.call-start = ((), (), s32[]{:S(2)}) async-start(), calls=%async_computation.6 | async-start | bytes 4718592 | tf_op jit(solution)/shard_map/reduce_scatter | solution.py:96
  233.9 2.4 copy-start.8
  244.5 0.7 copy-start.10
  244.5 0.7 copy-start.7
  333.1 6.0 %copy-start.6 = (f32[3,256]{1,0:T(4,128)S(1)}, f32[3,256]{1,0:T(4,128)}, u32[]{:S(2)}) copy-start(f32[3,256]{1,0:T(4,128)} %param.25) | copy-start | bytes 9220
  333.2 21.9 %all-to-all-start.1 = ((bf16[16,32,1024]{2,1,0:T(8,128)(2,1)}), bf16[16,32,1024]{2,1,0:T(8,128)(2,1)S(1)}, u32[]{:S(2)}, u32[]{:S(2)}) async-start(bf16[16,32,1024]{2,1,0:T(8,128)(2,1)} %copy.33), calls=%async_computation.3 | async-start | bytes 2097152 | tf_op jit(solution)/shard_map/all_to_all | solution.py:121
  360.5 10.8 %copy-start.3 = (bf16[3,3,256,256]{3,2,1,0:T(8,128)(2,1)S(1)}, bf16[3,3,256,256]{3,2,1,0:T(8,128)(2,1)}, u32[]{:S(2)}) copy-start(bf16[3,3,256,256]{3,2,1,0:T(8,128)(2,1)} %get-tuple-element.10) | copy-start | bytes 3538948
  362.1 9.9 %collective-permute-start = (bf16[1,256,256]{2,1,0:T(8,128)(2,1)S(1)}, bf16[1,256,256]{2,1,0:T(8,128)(2,1)S(1)}, u32[]{:S(2)}, u32[]{:S(2)}) collective-permute-start(bf16[1,256,256]{2,1,0:T(8,128)(2,1)S(1)} %get-tuple-element.19), channel_id=1, source_target_pairs={{0,1},{1,2},{2,3},{3,4},{4,5},{5,6},{6,7},{7,8},{8,9},{9,10},{10,1... | collective-permute-start | bytes 393224 | tf_op jit(solution)/shard_map/ppermute | solution.py:17
  365.0 9.5 %collective-permute-start.1 = (bf16[1,256,256]{2,1,0:T(8,128)(2,1)S(1)}, bf16[1,256,256]{2,1,0:T(8,128)(2,1)S(1)}, u32[]{:S(2)}, u32[]{:S(2)}) collective-permute-start(bf16[1,256,256]{2,1,0:T(8,128)(2,1)S(1)} %get-tuple-element.20), channel_id=1, source_target_pairs={{1,0},{2,1},{3,2},{4,3},{5,4},{6,5},{7,6},{8,7},{9,8},{10,9},{11,1... | collective-permute-start | bytes 393224 | tf_op jit(solution)/shard_map/ppermute | solution.py:20
  377.7 10.7 %collective-permute-start.2 = (bf16[1,256,256]{2,1,0:T(8,128)(2,1)S(1)}, bf16[1,256,256]{2,1,0:T(8,128)(2,1)S(1)}, u32[]{:S(2)}, u32[]{:S(2)}) collective-permute-start(bf16[1,256,256]{2,1,0:T(8,128)(2,1)S(1)} %get-tuple-element.17), channel_id=1, source_target_pairs={{0,1},{1,2},{2,3},{3,4},{4,5},{5,6},{6,7},{7,8},{8,9},{9,10},{10,1... | collective-permute-start | bytes 393224 | tf_op jit(solution)/shard_map/ppermute | solution.py:17
  379.7 11.0 %collective-permute-start.3 = (bf16[1,256,256]{2,1,0:T(8,128)(2,1)S(1)}, bf16[1,256,256]{2,1,0:T(8,128)(2,1)S(1)}, u32[]{:S(2)}, u32[]{:S(2)}) collective-permute-start(bf16[1,256,256]{2,1,0:T(8,128)(2,1)S(1)} %get-tuple-element.18), channel_id=1, source_target_pairs={{1,0},{2,1},{3,2},{4,3},{5,4},{6,5},{7,6},{8,7},{9,8},{10,9},{11,1... | collective-permute-start | bytes 393224 | tf_op jit(solution)/shard_map/ppermute | solution.py:20
  393.8 10.6 %collective-permute-start.4 = (bf16[1,256,256]{2,1,0:T(8,128)(2,1)S(1)}, bf16[1,256,256]{2,1,0:T(8,128)(2,1)S(1)}, u32[]{:S(2)}, u32[]{:S(2)}) collective-permute-start(bf16[1,256,256]{2,1,0:T(8,128)(2,1)S(1)} %get-tuple-element.15), channel_id=1, source_target_pairs={{0,1},{1,2},{2,3},{3,4},{4,5},{5,6},{6,7},{7,8},{8,9},{9,10},{10,1... | collective-permute-start | bytes 393224 | tf_op jit(solution)/shard_map/ppermute | solution.py:17
  395.7 10.9 %collective-permute-start.5 = (bf16[1,256,256]{2,1,0:T(8,128)(2,1)S(1)}, bf16[1,256,256]{2,1,0:T(8,128)(2,1)S(1)}, u32[]{:S(2)}, u32[]{:S(2)}) collective-permute-start(bf16[1,256,256]{2,1,0:T(8,128)(2,1)S(1)} %get-tuple-element.16), channel_id=1, source_target_pairs={{1,0},{2,1},{3,2},{4,3},{5,4},{6,5},{7,6},{8,7},{9,8},{10,9},{11,1... | collective-permute-start | bytes 393224 | tf_op jit(solution)/shard_map/ppermute | solution.py:20
  408.6 1.6 copy-start.1
Sparse Core Ops, SparseCore 0:
  11.5 74.3 all-gather.1
  99.7 81.8 reduce-scatter.2
  244.7 85.0 reduce-scatter.4
